TPU v7x, 32 devices: a whole 2x2x4 slice. The times are simulated.
32 devices in a mesh: dp: 8 (over z, y), mp: 4 (over x, core).
Axes of the slice: x: 2, y: 2, z: 4, core: 2. Of those that a mesh axis runs over, the one named last changes fastest.
Arguments:
- tokens: bfloat16 [4096, 1152], P(('dp', 'mp')), may hold values from -6 to 6
- segment_ids: int32 [4096], P('dp'), may hold values from 0 to 2, as said below
- positions: int32 [4096], P('dp'), may hold values from 0 to 5118, as said below
- q_weight: bfloat16 [1152, 1024], P('dp', 'mp'), may hold values from -0.1875 to 0.1875
- kv_weight: bfloat16 [1152, 512], P('dp'), may hold values from -0.1875 to 0.1875
- o_weight: bfloat16 [1024, 1152], P('mp', 'dp'), may hold values from -0.1875 to 0.1875
- gate_up_weight: bfloat16 [2, 1152, 6912], P(None, 'dp', 'mp'), may hold values from -0.1875 to 0.1875
- down_weight: bfloat16 [6912, 1152], P('mp', 'dp'), may hold values from -0.078125 to 0.078125
- attn_pre_gain: bfloat16 [1152], P('dp'), may hold values from 0.25 to 1.75
- attn_post_gain: bfloat16 [1152], P('dp'), may hold values from 0.25 to 1.75
- ff_pre_gain: bfloat16 [1152], P('dp'), may hold values from 0.25 to 1.75
- ff_post_gain: bfloat16 [1152], P('dp'), may hold values from 0.25 to 1.75
- query_gain: bfloat16 [256], P('dp'), may hold values from 0.25 to 1.75
- key_gain: bfloat16 [256], P('dp'), may hold values from 0.25 to 1.75
- out_grad: bfloat16 [4096, 1152], P(('dp', 'mp')), may hold values from -6 to 6
Outputs:
- out: bfloat16 [4096, 1152], P(('dp', 'mp'))
- tokens_grad: float32 [4096, 1152], P(('dp', 'mp'))
- q_weight_grad: float32 [1152, 1024], P('dp', 'mp')
- kv_weight_grad: float32 [1152, 512], P('dp')
- o_weight_grad: float32 [1024, 1152], P('mp', 'dp')
- gate_up_weight_grad: float32 [2, 1152, 6912], P(None, 'dp', 'mp')
- down_weight_grad: float32 [6912, 1152], P('mp', 'dp')
- attn_pre_gain_grad: float32 [1152], P('dp')
- attn_post_gain_grad: float32 [1152], P('dp')
- ff_pre_gain_grad: float32 [1152], P('dp')
- ff_post_gain_grad: float32 [1152], P('dp')
- query_gain_grad: float32 [256], P('dp')
- key_gain_grad: float32 [256], P('dp')
Inputs may be any that keep to these rules, and one draw needn't show every extreme that they name: `segment_ids`: segment ids never fall; document 0 and document 2 each hold 1 to 256 tokens, document 1 the rest. Within a document, positions rise by one from token to token; document 0 starts at position 0, document 2 at 0 to 1023, and the last token of document 1 has position 5118.
All inputs are finite; a program needn't handle non-finite values.
Results may differ from a plain program's by a relative error of at most 0.028.
Values may be sent and summed in bfloat16 or wider, within the bound.
A program may use at most 128 MiB of HBM per device.

v0:
```python
from functools import partial
import jax
import jax.numpy as jnp
from jax import lax
from jax.sharding import PartitionSpec as P

WINDOW = 512
EPS = 1e-06
NEG = -1e30


def from_behind(value, axis, steps):
    count = lax.axis_size(axis)
    leading, last = (max(0, -steps), min(count, count - steps))
    return lax.ppermute(value, axis, [(source, source + steps) for source in range(leading, last)])


def shifted(value, axis, shift):
    count = lax.axis_size(axis)
    return lax.ppermute(value, axis, [(i, (i + shift) % count) for i in range(count)])


def gather_relative(value):
    count = lax.axis_size("mp")
    return [value] + [shifted(value, "mp", -step) for step in range(1, count)]


def gather_ordered(value):
    count = lax.axis_size("mp")
    rows = value.shape[0]
    me = lax.axis_index("mp")
    whole = jnp.zeros((count * rows,) + value.shape[1:], value.dtype)
    for step, block in enumerate(gather_relative(value)):
        owner = lax.rem(me + step, count)
        whole = lax.dynamic_update_slice_in_dim(whole, block, owner * rows, axis=0)
    return whole


def scatter_relative(blocks):
    total = blocks[0].astype(jnp.float32)
    for step in range(1, len(blocks)):
        total = total + shifted(blocks[step], "mp", step).astype(jnp.float32)
    return total


def scatter_ordered(value):
    count = lax.axis_size("mp")
    rows = value.shape[0] // count
    me = lax.axis_index("mp")
    return scatter_relative(
        [
            lax.dynamic_slice_in_dim(value, lax.rem(me + step, count) * rows, rows, axis=0)
            for step in range(count)
        ]
    )


def split_rows(value):
    rows = value.shape[0] // lax.axis_size("mp")
    return [value[i * rows : (i + 1) * rows] for i in range(lax.axis_size("mp"))]


def sum_over_mp(value):
    total = value.astype(jnp.float32)
    for step in range(1, lax.axis_size("mp")):
        total = total + shifted(value, "mp", step).astype(jnp.float32)
    return total


def normalize(value, gain):
    return value * lax.rsqrt(jnp.mean(value * value, axis=-1, keepdims=True) + EPS) * gain


def rotary_tables(positions, width):
    half_width = width // 2
    frequency = jnp.power(10000.0, -jnp.arange(half_width, dtype=jnp.float32) * (2.0 / width))
    angles = positions.astype(jnp.float32)[:, None] * frequency[None, :]
    return (jnp.cos(angles), jnp.sin(angles))


def rotate(value, cosine, sine):
    half_width = value.shape[-1] // 2
    first_half = value[..., :half_width]
    second_half = value[..., half_width:]
    return jnp.concatenate(
        [first_half * cosine - second_half * sine, second_half * cosine + first_half * sine],
        axis=-1,
    )


def prepare_head(pre_value, gain, cosine, sine):
    return rotate(normalize(pre_value, gain), cosine, sine)


def gated_units(gate, up_part):
    return jax.nn.gelu(gate, approximate=True) * up_part


def norm_back(value, gain, grad):
    unused, pull = jax.vjp(normalize, value, gain)
    return pull(grad)


def local(
    tokens,
    segment_ids,
    positions,
    q_weight,
    kv_weight,
    o_weight,
    gate_up_weight,
    down_weight,
    attn_pre_gain,
    attn_post_gain,
    ff_pre_gain,
    ff_post_gain,
    query_gain,
    key_gain,
    out_grad,
):
    rows = q_weight.shape[0]
    head_size = q_weight.shape[1]
    width = rows * lax.axis_size("dp")
    gain_rows = query_gain.shape[0]
    small_gains = [jnp.pad(item, (0, rows - gain_rows)) for item in (query_gain, key_gain)]
    gain_columns = jnp.stack(
        [attn_pre_gain, attn_post_gain, ff_pre_gain, ff_post_gain] + small_gains, axis=1
    )
    gain_columns = jnp.pad(gain_columns, ((0, 0), (0, 128 - gain_columns.shape[1])))
    packed = jnp.concatenate([q_weight, kv_weight, jnp.transpose(o_weight), gain_columns], axis=1)
    packed_full = lax.all_gather(packed, "dp", axis=0, tiled=True)
    gate_up_full = lax.all_gather(gate_up_weight, "dp", axis=1, tiled=True)
    down_full = lax.all_gather(down_weight, "dp", axis=1, tiled=True)
    joint_weight = packed_full[:, : 3 * head_size]
    output_turned = packed_full[:, 3 * head_size : 4 * head_size]
    gain_block = jnp.transpose(packed_full[:, 4 * head_size :]).astype(jnp.float32)
    gains = [gain_block[i] for i in range(4)] + [
        gain_block[i].reshape(-1, rows)[:, :gain_rows].reshape(-1) for i in (4, 5)
    ]
    length = segment_ids.shape[0]
    reach = -(-WINDOW // length)
    block_size = min(512, length)
    score_scale = head_size ** (-0.5)
    span = block_size + WINDOW
    cosine, sine = rotary_tables(positions, head_size)
    distance = (
        jnp.arange(block_size, dtype=jnp.int32)[:, None]
        + WINDOW
        - jnp.arange(span, dtype=jnp.int32)[None, :]
    )
    inside = (distance >= 0) & (distance < WINDOW)
    residual = tokens.astype(jnp.float32)
    attn_local = normalize(residual, gains[0]).astype(jnp.bfloat16)
    attn_in = gather_ordered(attn_local)
    projected = jnp.dot(attn_in, joint_weight, preferred_element_type=jnp.float32)
    query_pre = projected[:, :head_size]
    key_pre = projected[:, head_size : 2 * head_size]
    value_pre = projected[:, 2 * head_size :]
    queries = prepare_head(query_pre, gains[4], cosine, sine).astype(jnp.bfloat16)
    keys = prepare_head(key_pre, gains[5], cosine, sine).astype(jnp.bfloat16)
    values = value_pre.astype(jnp.bfloat16)
    marks = (segment_ids + 1).astype(jnp.bfloat16)
    key_parts, value_parts, mark_parts = ([], [], [])
    step = 1
    moved = from_behind((keys, values, marks), "dp", step)
    key_parts.append(moved[0])
    value_parts.append(moved[1])
    mark_parts.append(moved[2])
    all_keys = jnp.concatenate(key_parts + [keys], axis=0)
    all_values = jnp.concatenate(value_parts + [values], axis=0)
    all_marks = jnp.concatenate(mark_parts + [marks], axis=0)

    def block_parts(start):
        first_key = start + reach * length - WINDOW
        visible = inside & (marks[:, None] == all_marks[None, :])
        product = (
            jnp.einsum("qd,kd->qk", queries, all_keys, preferred_element_type=jnp.float32)
            * score_scale
        )
        return (first_key, queries, all_keys, all_values, jnp.where(visible, product, NEG))

    mixed_parts, total_parts = ([], [])
    start = 0
    first_key, query_block, key_block, value_block, scores = block_parts(start)
    highest = jnp.max(scores, axis=-1, keepdims=True)
    expo = jnp.exp(scores - highest)
    denominator = jnp.sum(expo, axis=-1, keepdims=True)
    probs = (expo / denominator).astype(jnp.bfloat16)
    mixed_parts.append(jnp.dot(probs, value_block, preferred_element_type=jnp.float32))
    total_parts.append(highest + jnp.log(denominator))
    attended = mixed_parts[0].astype(jnp.bfloat16)
    log_totals = total_parts[0]
    attn_out = scatter_ordered(
        jnp.einsum("le,de->ld", attended, output_turned, preferred_element_type=jnp.float32).astype(
            jnp.bfloat16
        )
    )
    middle = residual + normalize(attn_out, gains[1])
    ff_local = normalize(middle, gains[2]).astype(jnp.bfloat16)
    ff_in = jnp.concatenate(gather_relative(ff_local), axis=0)
    gate = jnp.dot(ff_in, gate_up_full[0], preferred_element_type=jnp.float32)
    up_part = jnp.dot(ff_in, gate_up_full[1], preferred_element_type=jnp.float32)
    hidden = gated_units(gate, up_part).astype(jnp.bfloat16)
    ff_out = scatter_relative(
        split_rows(
            jnp.dot(hidden, down_full, preferred_element_type=jnp.float32).astype(jnp.bfloat16)
        )
    )
    result = (middle + normalize(ff_out, gains[3])).astype(jnp.bfloat16)
    top_grad = out_grad.astype(jnp.float32)
    ff_out_grad, ff_post_grad = norm_back(ff_out, gains[3], top_grad)
    ff_grad_all = jnp.concatenate(gather_relative(ff_out_grad.astype(jnp.bfloat16)), axis=0)
    hidden_grad = jnp.einsum(
        "ld,fd->lf", ff_grad_all, down_full, preferred_element_type=jnp.float32
    )
    down_grad_turned = jnp.einsum(
        "ld,lf->df", ff_grad_all, hidden, preferred_element_type=jnp.float32
    )
    unused, unit_pull = jax.vjp(gated_units, gate, up_part)
    gate_grad, up_grad = unit_pull(hidden_grad)
    gate_low = gate_grad.astype(jnp.bfloat16)
    up_low = up_grad.astype(jnp.bfloat16)
    gate_turned = jnp.einsum("ld,lf->df", ff_in, gate_low, preferred_element_type=jnp.float32)
    up_turned = jnp.einsum("ld,lf->df", ff_in, up_low, preferred_element_type=jnp.float32)
    ff_in_partial = (
        jnp.einsum("lf,df->ld", gate_low, gate_up_full[0], preferred_element_type=jnp.float32)
        + jnp.einsum("lf,df->ld", up_low, gate_up_full[1], preferred_element_type=jnp.float32)
    ).astype(jnp.bfloat16)
    ff_in_partial, down_low, gate_turned_low, up_turned_low = lax.optimization_barrier(
        (
            ff_in_partial,
            down_grad_turned.astype(jnp.bfloat16),
            gate_turned.astype(jnp.bfloat16),
            up_turned.astype(jnp.bfloat16),
        )
    )
    feed_forward_owned = tuple(
        (
            lax.psum_scatter(item, "dp", scatter_dimension=0, tiled=True)
            for item in (down_low, gate_turned_low, up_turned_low)
        )
    )
    ff_in_grad = scatter_relative(split_rows(ff_in_partial))
    middle_part, ff_pre_grad = norm_back(middle, gains[2], ff_in_grad)
    middle_grad = top_grad + middle_part
    attn_out_grad, attn_post_grad = norm_back(attn_out, gains[1], middle_grad)
    attn_grad_all = gather_ordered(attn_out_grad.astype(jnp.bfloat16))
    attended_grad = jnp.einsum(
        "ld,de->le", attn_grad_all, output_turned, preferred_element_type=jnp.float32
    ).astype(jnp.bfloat16)
    output_grad_turned = jnp.einsum(
        "ld,le->de", attn_grad_all, attended, preferred_element_type=jnp.float32
    )
    key_grad_all = jnp.zeros(((reach + 1) * length, head_size), jnp.float32)
    value_grad_all = jnp.zeros(((reach + 1) * length, head_size), jnp.float32)
    start = 0
    first_key, query_block, key_block, value_block, scores = block_parts(start)
    probs = jnp.exp(scores - log_totals)
    probs_low = probs.astype(jnp.bfloat16)
    value_grad_all = value_grad_all.at[first_key : first_key + span].add(
        jnp.einsum("qk,qd->kd", probs_low, attended_grad, preferred_element_type=jnp.float32)
    )
    prob_grad = jnp.einsum(
        "qd,kd->qk", attended_grad, value_block, preferred_element_type=jnp.float32
    )
    inner = jnp.sum(probs * prob_grad, axis=-1, keepdims=True)
    score_grad = (probs * (prob_grad - inner)).astype(jnp.bfloat16)
    query_parts = jnp.dot(score_grad, key_block, preferred_element_type=jnp.float32) * score_scale
    key_grad_all = key_grad_all.at[first_key : first_key + span].add(
        jnp.einsum("qk,qd->kd", score_grad, query_block, preferred_element_type=jnp.float32)
        * score_scale
    )
    own_keys = key_grad_all[reach * length :]
    own_values = value_grad_all[reach * length :]
    step = 1
    slot = reach - step
    returned = (
        from_behind(
            key_grad_all[slot * length : (slot + 1) * length].astype(jnp.bfloat16), "dp", -step
        ).astype(jnp.float32),
        from_behind(
            value_grad_all[slot * length : (slot + 1) * length].astype(jnp.bfloat16), "dp", -step
        ).astype(jnp.float32),
    )
    own_keys = own_keys + returned[0]
    own_values = own_values + returned[1]
    unused, query_pull = jax.vjp(
        partial(prepare_head, cosine=cosine, sine=sine), query_pre, gains[4]
    )
    query_pre_grad, query_gain_grad = query_pull(query_parts)
    unused, key_pull = jax.vjp(partial(prepare_head, cosine=cosine, sine=sine), key_pre, gains[5])
    key_pre_grad, key_gain_grad = key_pull(own_keys)
    joint_grad_rows = jnp.concatenate([query_pre_grad, key_pre_grad, own_values], axis=1).astype(
        jnp.bfloat16
    )
    joint_grad = jnp.einsum(
        "ld,lc->dc", attn_in, joint_grad_rows, preferred_element_type=jnp.float32
    )
    attn_in_grad = scatter_ordered(
        jnp.einsum(
            "lc,dc->ld", joint_grad_rows, joint_weight, preferred_element_type=jnp.float32
        ).astype(jnp.bfloat16)
    )
    tokens_part, attn_pre_grad = norm_back(residual, gains[0], attn_in_grad)
    tokens_grad = middle_grad + tokens_part
    small_grads = [
        jnp.pad(item.reshape(-1, gain_rows), ((0, 0), (0, rows - gain_rows))).reshape(-1)
        for item in (query_gain_grad, key_gain_grad)
    ]
    gain_grads = jnp.stack(
        [attn_pre_grad, attn_post_grad, ff_pre_grad, ff_post_grad] + small_grads, axis=1
    )
    gain_grads = jnp.pad(gain_grads, ((0, 0), (0, 128 - gain_grads.shape[1])))
    packed_grad = jnp.concatenate(
        [
            joint_grad[:, :head_size].astype(jnp.bfloat16),
            output_grad_turned.astype(jnp.bfloat16),
            joint_grad[:, head_size:].astype(jnp.bfloat16),
            gain_grads.astype(jnp.bfloat16),
        ],
        axis=1,
    )
    packed_grad, feed_forward_owned = lax.optimization_barrier((packed_grad, feed_forward_owned))
    down_owned = jnp.transpose(feed_forward_owned[0]).astype(jnp.float32)
    gate_up_owned = jnp.stack(feed_forward_owned[1:], axis=0).astype(jnp.float32)
    packed_owned = lax.psum_scatter(packed_grad, "dp", scatter_dimension=0, tiled=True)
    query_owned = packed_owned[:, :head_size].astype(jnp.float32)
    output_owned = jnp.transpose(packed_owned[:, head_size : 2 * head_size]).astype(jnp.float32)
    summed = sum_over_mp(packed_owned[:, 2 * head_size :])
    keyval_owned = summed[:, : 2 * head_size]
    gain_owned = jnp.transpose(summed[:, 2 * head_size :])
    return (
        result,
        tokens_grad,
        query_owned,
        keyval_owned,
        output_owned,
        gate_up_owned,
        down_owned,
        gain_owned[0],
        gain_owned[1],
        gain_owned[2],
        gain_owned[3],
        gain_owned[4, :gain_rows],
        gain_owned[5, :gain_rows],
    )


def solution(mesh):
    placed = (
        P(("dp", "mp"), None),
        P("dp"),
        P("dp"),
        P("dp", "mp"),
        P("dp", None),
        P("mp", "dp"),
        P(None, "dp", "mp"),
        P("mp", "dp"),
        P("dp"),
        P("dp"),
        P("dp"),
        P("dp"),
        P("dp"),
        P("dp"),
        P(("dp", "mp"), None),
    )
    return jax.shard_map(
        local,
        mesh=mesh,
        in_specs=placed,
        out_specs=(
            P(("dp", "mp"), None),
            P(("dp", "mp"), None),
            P("dp", "mp"),
            P("dp", None),
            P("mp", "dp"),
            P(None, "dp", "mp"),
            P("mp", "dp"),
            P("dp"),
            P("dp"),
            P("dp"),
            P("dp"),
            P("dp"),
            P("dp"),
        ),
        check_vma=False,
    )
```

profile of v0, /device:TPU:0, one launch (start us, length us, event | category | flops | bytes accessed | tf_op | source)
XLA Modules:
  0.0 732.3 jit_solution(13621012869615528322)
XLA Ops:
  14.2 56.9 %all-gather.4.cloned.1.call-done = bf16[1152,1152]{1,0:T(8,128)(2,1)} async-done(((bf16[144,1152]{1,0:T(8,128)(2,1)}), bf16[1152,1152]{1,0:T(8,128)(2,1)}) %all-gather.4.cloned.1.call-update) | async-done | bytes 2654224 | tf_op jit(solution)/shard_map/all_gather | solution.py:131
  80.4 9.1 %collective-permute-done.2 = bf16[128,1152]{1,0:T(8,128)(2,1)S(1)} collective-permute-done((bf16[128,1152]{1,0:T(8,128)(2,1)S(1)}, bf16[128,1152]{1,0:T(8,128)(2,1)S(1)}, u32[]{:S(2)}, u32[]{:S(2)}) %collective-permute-start.2) | collective-permute-done | bytes 294944 | tf_op jit(solution)/shard_map/ppermute | solution.py:20
  103.1 10.1 %collective-permute-start.5 = (bf16[512,256]{1,0:T(8,128)(2,1)S(1)}, bf16[512,256]{1,0:T(8,128)(2,1)S(1)}, u32[]{:S(2)}, u32[]{:S(2)}) collective-permute-start(bf16[512,256]{1,0:T(8,128)(2,1)S(1)} %slice.321), channel_id=1, source_target_pairs={{0,4},{4,8},{8,12},{12,16},{16,20},{20,24},{24,28},{1,5},{5,9},{9,... | collective-permute-start | bytes 786440 | tf_op jit(solution)/shard_map/ppermute | solution.py:15
  120.8 5.7 collective-permute-done.8
  126.5 7.6 %collective-permute-done.7 = bf16[128,1152]{1,0:T(8,128)(2,1)S(1)} collective-permute-done((bf16[128,1152]{1,0:T(8,128)(2,1)S(1)}, bf16[128,1152]{1,0:T(8,128)(2,1)S(1)}, u32[]{:S(2)}, u32[]{:S(2)}) %collective-permute-start.7) | collective-permute-done | bytes 294944 | tf_op jit(solution)/shard_map/ppermute | solution.py:20
  138.2 6.0 collective-permute-done.11
  149.7 54.7 %all-gather.6.cloned.1.call-done = bf16[2,1152,1728]{2,1,0:T(8,128)(2,1)} async-done(((bf16[2,144,1728]{2,1,0:T(8,128)(2,1)}), bf16[2,1152,1728]{2,1,0:T(8,128)(2,1)}) %all-gather.6.cloned.1.call-update) | async-done | bytes 7962640 | tf_op jit(solution)/shard_map/all_gather | solution.py:132
  211.4 6.8 multiply_convert_fusion.1
  218.2 59.2 %all-gather.8.cloned.1.call-done = bf16[1728,1152]{0,1:T(8,128)(2,1)} async-done(((bf16[1728,144]{0,1:T(8,128)(2,1)}), bf16[1728,1152]{0,1:T(8,128)(2,1)}) %all-gather.8.cloned.1.call-update) | async-done | bytes 3981328 | tf_op jit(solution)/shard_map/all_gather | solution.py:133
  277.4 5.3 convolution_convert_fusion.5
  289.2 9.2 %collective-permute-done.13 = bf16[128,1152]{1,0:T(8,128)(2,1)S(1)} collective-permute-done((bf16[128,1152]{1,0:T(8,128)(2,1)S(1)}, bf16[128,1152]{1,0:T(8,128)(2,1)S(1)}, u32[]{:S(2)}, u32[]{:S(2)}) %collective-permute-start.13) | collective-permute-done | bytes 294944 | tf_op jit(solution)/shard_map/ppermute | solution.py:20
  302.6 6.7 collective-permute-done.17
  318.6 8.4 %multiply_convert_fusion = (bf16[512,1728]{0,1:T(8,128)(2,1)S(1)}, bf16[512,1728]{0,1:T(8,128)(2,1)S(1)}) fusion(f32[512,1728]{0,1:T(8,128)S(1)} %copy-done.77, f32[512,1728]{0,1:T(8,128)} %get-tuple-element.185, bf16[1728,1152]{0,1:T(8,128)(2,1)S(1)} %copy-done.67, bf16[128,1152]{1,0:T(8,128)(2,1)S(1)} %collective-permute-done.17, ...), kind=kOutput, calls=%fused_computation.20 | convolution fusion | flops 2064384000 | bytes 15777792 | tf_op jit(solution)/shard_map/ld,fd->lf/dot_general | solution.py:213
  329.7 5.4 convolution_convert_fusion.1
  344.1 6.5 copy.60
  350.7 6.5 copy.62
  362.7 6.5 copy.64
  369.2 7.4 %collective-permute-done.19 = bf16[128,1152]{1,0:T(8,128)(2,1)} collective-permute-done((bf16[128,1152]{1,0:T(8,128)(2,1)}, bf16[128,1152]{1,0:T(8,128)(2,1)}, u32[]{:S(2)}, u32[]{:S(2)}) %collective-permute-start.19) | collective-permute-done | bytes 294944 | tf_op jit(solution)/shard_map/ppermute | solution.py:20
  388.4 6.6 collective-permute-done.22
  403.9 13.7 %collective-permute-done.24 = bf16[512,256]{1,0:T(8,128)(2,1)S(1)} collective-permute-done((bf16[512,256]{1,0:T(8,128)(2,1)S(1)}, bf16[512,256]{1,0:T(8,128)(2,1)S(1)}, u32[]{:S(2)}, u32[]{:S(2)}) %collective-permute-start.24) | collective-permute-done | bytes 262176 | tf_op jit(solution)/shard_map/ppermute | solution.py:15
  449.0 89.0 %reduce-scatter.15.cloned.1.call-done = bf16[144,1728]{1,0:T(8,128)(2,1)} async-done(((bf16[1152,1728]{1,0:T(8,128)(2,1)}), bf16[144,1728]{1,0:T(8,128)(2,1)}) %reduce-scatter.15.cloned.1.call-update) | async-done | bytes 497680
  540.2 88.7 %reduce-scatter.17.cloned.1.call-done = bf16[144,1728]{1,0:T(8,128)(2,1)} async-done(((bf16[1152,1728]{1,0:T(8,128)(2,1)}), bf16[144,1728]{1,0:T(8,128)(2,1)}) %reduce-scatter.17.cloned.1.call-update) | async-done | bytes 497680
  642.2 62.7 %reduce-scatter.19.cloned.1.call-done = bf16[144,1152]{1,0:T(8,128)(2,1)} async-done(((bf16[1152,1152]{1,0:T(8,128)(2,1)}), bf16[144,1152]{1,0:T(8,128)(2,1)}) %reduce-scatter.19.cloned.1.call-update) | async-done | bytes 331792
  713.1 9.9 %collective-permute-done.30 = bf16[144,640]{0,1:T(8,128)(2,1)S(1)} collective-permute-done((bf16[144,640]{0,1:T(8,128)(2,1)S(1)}, bf16[144,640]{0,1:T(8,128)(2,1)S(1)}, u32[]{:S(2)}, u32[]{:S(2)}) %collective-permute-start.30) | collective-permute-done | bytes 184352 | tf_op jit(solution)/shard_map/ppermute | solution.py:20
  (360 shorter events, 168.2 us)
Async XLA Ops:
  7.2 63.9 %all-gather.4.cloned.1.call-start = ((), (), s32[]{:S(2)}) async-start(), calls=%async_computation.4 | async-start | bytes 2985984 | tf_op jit(solution)/shard_map/all_gather | solution.py:131
  13.2 191.2 %all-gather.6.cloned.1.call-start = ((), (), s32[]{:S(2)}) async-start(), calls=%async_computation.5 | async-start | bytes 9289728 | tf_op jit(solution)/shard_map/all_gather | solution.py:132
  13.9 263.5 %all-gather.8.cloned.1.call-start = ((), (), s32[]{:S(2)}) async-start(), calls=%async_computation.6 | async-start | bytes 4644864 | tf_op jit(solution)/shard_map/all_gather | solution.py:133
  74.2 372.5 %reduce-scatter.13.cloned.1.call-start = ((), (), s32[]{:S(2)}) async-start(), calls=%async_computation.7 | async-start | bytes 4644864
  74.5 15.0 %collective-permute-start.2 = (bf16[128,1152]{1,0:T(8,128)(2,1)S(1)}, bf16[128,1152]{1,0:T(8,128)(2,1)S(1)}, u32[]{:S(2)}, u32[]{:S(2)}) collective-permute-start(bf16[128,1152]{1,0:T(8,128)(2,1)S(1)} %get-tuple-element.141), channel_id=1, source_target_pairs={{0,2},{1,3},{2,0},{3,1},{4,6},{5,7},{6,4},{7,5},{8,10},{9,11},{10,... | collective-permute-start | bytes 884744 | tf_op jit(solution)/shard_map/ppermute | solution.py:20
  76.0 13.8 %collective-permute-start.3 = (bf16[128,1152]{1,0:T(8,128)(2,1)S(1)}, bf16[128,1152]{1,0:T(8,128)(2,1)S(1)}, u32[]{:S(2)}, u32[]{:S(2)}) collective-permute-start(bf16[128,1152]{1,0:T(8,128)(2,1)S(1)} %get-tuple-element.141), channel_id=1, source_target_pairs={{0,1},{1,2},{2,3},{3,0},{4,5},{5,6},{6,7},{7,4},{8,9},{9,10},{10,1... | collective-permute-start | bytes 884744 | tf_op jit(solution)/shard_map/ppermute | solution.py:20
  94.9 18.2 %collective-permute-start.4 = (bf16[512,256]{1,0:T(8,128)(2,1)S(1)}, bf16[512,256]{1,0:T(8,128)(2,1)S(1)}, u32[]{:S(2)}, u32[]{:S(2)}) collective-permute-start(bf16[512,256]{1,0:T(8,128)(2,1)S(1)} %pad_maximum_fusion.9), channel_id=1, source_target_pairs={{0,4},{4,8},{8,12},{12,16},{16,20},{20,24},{24,28},{1,5},{5,9},{9,... | collective-permute-start | bytes 786440 | tf_op jit(solution)/shard_map/ppermute | solution.py:15
  103.1 13.9 %collective-permute-start.5 = (bf16[512,256]{1,0:T(8,128)(2,1)S(1)}, bf16[512,256]{1,0:T(8,128)(2,1)S(1)}, u32[]{:S(2)}, u32[]{:S(2)}) collective-permute-start(bf16[512,256]{1,0:T(8,128)(2,1)S(1)} %slice.321), channel_id=1, source_target_pairs={{0,4},{4,8},{8,12},{12,16},{16,20},{20,24},{24,28},{1,5},{5,9},{9,... | collective-permute-start | bytes 786440 | tf_op jit(solution)/shard_map/ppermute | solution.py:15
  119.6 14.6 %collective-permute-start.7 = (bf16[128,1152]{1,0:T(8,128)(2,1)S(1)}, bf16[128,1152]{1,0:T(8,128)(2,1)S(1)}, u32[]{:S(2)}, u32[]{:S(2)}) collective-permute-start(bf16[128,1152]{1,0:T(8,128)(2,1)S(1)} %get-tuple-element.159), channel_id=1, source_target_pairs={{0,2},{1,3},{2,0},{3,1},{4,6},{5,7},{6,4},{7,5},{8,10},{9,11},{10,... | collective-permute-start | bytes 884744 | tf_op jit(solution)/shard_map/ppermute | solution.py:20
  120.6 14.1 %collective-permute-start.6 = (bf16[128,1152]{1,0:T(8,128)(2,1)S(1)}, bf16[128,1152]{1,0:T(8,128)(2,1)S(1)}, u32[]{:S(2)}, u32[]{:S(2)}) collective-permute-start(bf16[128,1152]{1,0:T(8,128)(2,1)S(1)} %get-tuple-element.157), channel_id=1, source_target_pairs={{0,1},{1,2},{2,3},{3,0},{4,5},{5,6},{6,7},{7,4},{8,9},{9,10},{10,1... | collective-permute-start | bytes 884744 | tf_op jit(solution)/shard_map/ppermute | solution.py:20
  282.9 15.5 %collective-permute-start.13 = (bf16[128,1152]{1,0:T(8,128)(2,1)S(1)}, bf16[128,1152]{1,0:T(8,128)(2,1)S(1)}, u32[]{:S(2)}, u32[]{:S(2)}) collective-permute-start(bf16[128,1152]{1,0:T(8,128)(2,1)S(1)} %get-tuple-element.156), channel_id=1, source_target_pairs={{0,2},{1,3},{2,0},{3,1},{4,6},{5,7},{6,4},{7,5},{8,10},{9,11},{10,... | collective-permute-start | bytes 884744 | tf_op jit(solution)/shard_map/ppermute | solution.py:20
  284.4 14.1 %collective-permute-start.12 = (bf16[128,1152]{1,0:T(8,128)(2,1)S(1)}, bf16[128,1152]{1,0:T(8,128)(2,1)S(1)}, u32[]{:S(2)}, u32[]{:S(2)}) collective-permute-start(bf16[128,1152]{1,0:T(8,128)(2,1)S(1)} %get-tuple-element.154), channel_id=1, source_target_pairs={{0,1},{1,2},{2,3},{3,0},{4,5},{5,6},{6,7},{7,4},{8,9},{9,10},{10,1... | collective-permute-start | bytes 884744 | tf_op jit(solution)/shard_map/ppermute | solution.py:20
  350.6 187.4 %reduce-scatter.15.cloned.1.call-start = ((), (), s32[]{:S(2)}) async-start(), calls=%async_computation.8 | async-start | bytes 4644864
  357.2 271.7 %reduce-scatter.17.cloned.1.call-start = ((), (), s32[]{:S(2)}) async-start(), calls=%async_computation.9 | async-start | bytes 4644864
  361.2 15.4 %collective-permute-start.19 = (bf16[128,1152]{1,0:T(8,128)(2,1)}, bf16[128,1152]{1,0:T(8,128)(2,1)}, u32[]{:S(2)}, u32[]{:S(2)}) collective-permute-start(bf16[128,1152]{1,0:T(8,128)(2,1)} %get-tuple-element.153), channel_id=1, source_target_pairs={{0,2},{1,3},{2,0},{3,1},{4,6},{5,7},{6,4},{7,5},{8,10},{9,11},{10,... | collective-permute-start | bytes 884744 | tf_op jit(solution)/shard_map/ppermute | solution.py:20
  362.7 14.0 %collective-permute-start.18 = (bf16[128,1152]{1,0:T(8,128)(2,1)}, bf16[128,1152]{1,0:T(8,128)(2,1)}, u32[]{:S(2)}, u32[]{:S(2)}) collective-permute-start(bf16[128,1152]{1,0:T(8,128)(2,1)} %get-tuple-element.151), channel_id=1, source_target_pairs={{0,1},{1,2},{2,3},{3,0},{4,5},{5,6},{6,7},{7,4},{8,9},{9,10},{10,1... | collective-permute-start | bytes 884744 | tf_op jit(solution)/shard_map/ppermute | solution.py:20
  369.2 335.7 %reduce-scatter.19.cloned.1.call-start = ((), (), s32[]{:S(2)}) async-start(), calls=%async_computation.10 | async-start | bytes 2985984
  381.2 13.8 %collective-permute-start.22 = (bf16[128,1152]{1,0:T(8,128)(2,1)S(1)}, bf16[128,1152]{1,0:T(8,128)(2,1)S(1)}, u32[]{:S(2)}, u32[]{:S(2)}) collective-permute-start(bf16[128,1152]{1,0:T(8,128)(2,1)S(1)} %get-tuple-element.132), channel_id=1, source_target_pairs={{0,2},{1,3},{2,0},{3,1},{4,6},{5,7},{6,4},{7,5},{8,10},{9,11},{10,... | collective-permute-start | bytes 884744 | tf_op jit(solution)/shard_map/ppermute | solution.py:20
  381.9 14.1 %collective-permute-start.23 = (bf16[128,1152]{1,0:T(8,128)(2,1)S(1)}, bf16[128,1152]{1,0:T(8,128)(2,1)S(1)}, u32[]{:S(2)}, u32[]{:S(2)}) collective-permute-start(bf16[128,1152]{1,0:T(8,128)(2,1)S(1)} %get-tuple-element.132), channel_id=1, source_target_pairs={{0,1},{1,2},{2,3},{3,0},{4,5},{5,6},{6,7},{7,4},{8,9},{9,10},{10,1... | collective-permute-start | bytes 884744 | tf_op jit(solution)/shard_map/ppermute | solution.py:20
  397.2 22.6 %collective-permute-start.25 = (bf16[512,256]{1,0:T(8,128)(2,1)S(1)}, bf16[512,256]{1,0:T(8,128)(2,1)S(1)}, u32[]{:S(2)}, u32[]{:S(2)}) collective-permute-start(bf16[512,256]{1,0:T(8,128)(2,1)S(1)} %slice.319), channel_id=1, source_target_pairs={{4,0},{8,4},{12,8},{16,12},{20,16},{24,20},{28,24},{5,1},{9,5},{13... | collective-permute-start | bytes 786440 | tf_op jit(solution)/shard_map/ppermute | solution.py:15
  400.6 16.9 %collective-permute-start.24 = (bf16[512,256]{1,0:T(8,128)(2,1)S(1)}, bf16[512,256]{1,0:T(8,128)(2,1)S(1)}, u32[]{:S(2)}, u32[]{:S(2)}) collective-permute-start(bf16[512,256]{1,0:T(8,128)(2,1)S(1)} %slice.320), channel_id=1, source_target_pairs={{4,0},{8,4},{12,8},{16,12},{20,16},{24,20},{28,24},{5,1},{9,5},{13... | collective-permute-start | bytes 786440 | tf_op jit(solution)/shard_map/ppermute | solution.py:15
  422.3 14.2 %collective-permute-start.26 = (bf16[128,1152]{1,0:T(8,128)(2,1)S(1)}, bf16[128,1152]{1,0:T(8,128)(2,1)}, u32[]{:S(2)}, u32[]{:S(2)}) collective-permute-start(bf16[128,1152]{1,0:T(8,128)(2,1)S(1)} %get-tuple-element.148), channel_id=1, source_target_pairs={{0,1},{1,2},{2,3},{3,0},{4,5},{5,6},{6,7},{7,4},{8,9},{9,10},{10,1... | collective-permute-start | bytes 884744 | tf_op jit(solution)/shard_map/ppermute | solution.py:20
  706.1 16.9 %collective-permute-start.30 = (bf16[144,640]{0,1:T(8,128)(2,1)S(1)}, bf16[144,640]{0,1:T(8,128)(2,1)S(1)}, u32[]{:S(2)}, u32[]{:S(2)}) collective-permute-start(bf16[144,640]{0,1:T(8,128)(2,1)S(1)} %copy.69), channel_id=1, source_target_pairs={{0,2},{1,3},{2,0},{3,1},{4,6},{5,7},{6,4},{7,5},{8,10},{9,11},{10,... | collective-permute-start | bytes 552968 | tf_op jit(solution)/shard_map/ppermute | solution.py:20
  707.6 15.5 %collective-permute-start.29 = (bf16[144,640]{0,1:T(8,128)(2,1)S(1)}, bf16[144,640]{0,1:T(8,128)(2,1)S(1)}, u32[]{:S(2)}, u32[]{:S(2)}) collective-permute-start(bf16[144,640]{0,1:T(8,128)(2,1)S(1)} %copy.69), channel_id=1, source_target_pairs={{0,1},{1,2},{2,3},{3,0},{4,5},{5,6},{6,7},{7,4},{8,9},{9,10},{10,1... | collective-permute-start | bytes 552968 | tf_op jit(solution)/shard_map/ppermute | solution.py:20
  (97 other events, 906.3 us)
Sparse Core Ops, SparseCore 0:
  13.3 57.7 all-gather.3
  73.3 131.1 all-gather.5
  206.6 70.7 all-gather.7
  350.7 95.9 reduce-scatter.12
  450.5 87.4 reduce-scatter.14
  541.4 87.4 reduce-scatter.16
  634.6 70.2 reduce-scatter.18
where the time goes:
time: 740 us; the launch traced here: 732 us
  waiting for transfers between devices  533 us (72%)
  local copies, waits for them, and re-layouts  65.2 us (9%)
  matrix products  59.8 us (8%)
  starting transfers between devices  36.2 us (5%)
  other arithmetic  22.5 us (3%)
  between operations  15.8 us (2%)
    unnamed x11, waiting for transfers between devices  246 us
    ppermute x27, waiting for transfers between devices, shifted(): lax.ppermute(value, axis, [(i, (i + shift) % count) for i in range(count)])  99.2 us
    all_gather x1, waiting for transfers between devices, local(): down_full = lax.all_gather(down_weight, 'dp', axis=1, tiled=True)  59.2 us
    all_gather x1, waiting for transfers between devices, local(): packed_full = lax.all_gather(packed, 'dp', axis=0, tiled=True)  56.9 us
    all_gather x1, waiting for transfers between devices, local(): gate_up_full = lax.all_gather(gate_up_weight, 'dp', axis=1, tiled=True)  54.7 us
    unnamed x175, local copies, waits for them, and re-layouts  34.6 us
    ppermute x5, starting transfers between devices, from_behind(): lax.ppermute(value, axis, [(source, source + steps) for source in range(l...  19.4 us
    ppermute x5, waiting for transfers between devices, from_behind(): lax.ppermute(value, axis, [(source, source + steps) for source in range(l...  17.3 us
  transfers between devices with their start and end apart: 39, of which 34 were waited for; matrix products, arithmetic and copies ran while one was open for 11% of the time, Pallas kernels for 0%

commit v1 on v0

--- a/solution.py
+++ b/solution.py
@@ -7,6 +7,28 @@
 WINDOW = 512
 EPS = 1e-06
 NEG = -1e30
+
+
+def joined_along(blocks, dim):
+    lengths = list(blocks.shape[1:])
+    lengths[dim] *= blocks.shape[0]
+    return jnp.moveaxis(blocks, 0, dim).reshape(lengths)
+
+
+def collect(x, axis, dim):
+    size = lax.axis_size(axis)
+    pairs = [(i, (i + 1) % size) for i in range(size)]
+    back = [(b, a) for a, b in pairs]
+    lower, upper = ([], [])
+    for lap in range(size - 1):
+        if lap % 2 == 0:
+            lower.append(lax.ppermute(lower[-1] if lower else x, axis, pairs))
+        else:
+            upper.append(lax.ppermute(upper[-1] if upper else x, axis, back))
+    blocks = jnp.stack([*lower[::-1], x, *upper])
+    shift = lax.axis_index(axis) - len(lower)
+    blocks = blocks[(jnp.arange(size) - shift) % size]
+    return joined_along(blocks, dim)
 
 
 def from_behind(value, axis, steps):
@@ -129,7 +151,7 @@
     gain_columns = jnp.pad(gain_columns, ((0, 0), (0, 128 - gain_columns.shape[1])))
     packed = jnp.concatenate([q_weight, kv_weight, jnp.transpose(o_weight), gain_columns], axis=1)
     packed_full = lax.all_gather(packed, "dp", axis=0, tiled=True)
-    gate_up_full = lax.all_gather(gate_up_weight, "dp", axis=1, tiled=True)
+    gate_up_full = collect(gate_up_weight, "dp", 1)
     down_full = lax.all_gather(down_weight, "dp", axis=1, tiled=True)
     joint_weight = packed_full[:, : 3 * head_size]
     output_turned = packed_full[:, 3 * head_size : 4 * head_size]

time: 740 us -> 759 us (1.026)
  local copies, waits for them, and re-layouts: 65.2 us -> 91.8 us
  waiting for transfers between devices: 533 us -> 519 us
    ppermute x0 -> x7, waiting for transfers between devices: none -> 137 us  [the longest x4 137 us: collect(): lower.append(lax.ppermute(lower[-1] if lower else x, axis, pairs))]
    all_gather x1, waiting for transfers between devices: 59.2 us -> 0.01 us  [local(): down_full = lax.all_gather(down_weight, 'dp', axis=1, tiled=True)]
    all_gather x1, waiting for transfers between devices: 56.9 us -> 0.01 us  [local(): packed_full = lax.all_gather(packed, 'dp', axis=0, tiled=True)]
    all_gather x1 -> x0, waiting for transfers between devices: 54.7 us -> none  [local(): gate_up_full = lax.all_gather(gate_up_weight, 'dp', axis=1, tiled=True)]
    ppermute x5, waiting for transfers between devices: 17.3 us -> 50.9 us  [from_behind(): lax.ppermute(value, axis, [(source, source + steps) for source in range(l...]
    ppermute x0 -> x7, starting transfers between devices: none -> 16.2 us  [the longest x3 8.14 us: collect(): upper.append(lax.ppermute(upper[-1] if upper else x, axis, back))]
    ppermute x27, waiting for transfers between devices: 99.2 us -> 85.2 us  [shifted(): lax.ppermute(value, axis, [(i, (i + shift) % count) for i in range(count)])]
    unnamed x175 -> x182, local copies, waits for them, and re-layouts: 34.6 us -> 47.3 us
  transfers between devices with their start and end apart: 39 -> 45, of which waited for: 34 -> 34; matrix products, arithmetic and copies ran while one was open for 11% -> 15% of each run, Pallas kernels for 0% -> 0%
where the time goes in v1:
time: 759 us; the launch traced here: 750 us
  waiting for transfers between devices  519 us (68%)
  local copies, waits for them, and re-layouts  91.8 us (12%)
  matrix products  53.2 us (7%)
  starting transfers between devices  43.5 us (6%)
  other arithmetic  27 us (4%)
  between operations  15.7 us (2%)
    unnamed x10, waiting for transfers between devices  245 us
    ppermute x4, waiting for transfers between devices, collect(): lower.append(lax.ppermute(lower[-1] if lower else x, axis, pairs))  137 us
    ppermute x27, waiting for transfers between devices, shifted(): lax.ppermute(value, axis, [(i, (i + shift) % count) for i in range(count)])  85.2 us
    ppermute x5, waiting for transfers between devices, from_behind(): lax.ppermute(value, axis, [(source, source + steps) for source in range(l...  50.9 us
    unnamed x182, local copies, waits for them, and re-layouts  47.3 us
    ppermute x27, starting transfers between devices, shifted(): lax.ppermute(value, axis, [(i, (i + shift) % count) for i in range(count)])  16.6 us
  transfers between devices with their start and end apart: 45, of which 34 were waited for; matrix products, arithmetic and copies ran while one was open for 15% of the time, Pallas kernels for 0%

profile of v1, /device:TPU:0, one launch (start us, length us, event | category | flops | bytes accessed | tf_op | source)
XLA Modules:
  0.0 749.9 jit_solution(10566087925165221907)
XLA Ops:
  16.2 36.8 %collective-permute-done.12 = bf16[2,144,1728]{2,1,0:T(8,128)(2,1)S(1)} collective-permute-done((bf16[2,144,1728]{2,1,0:T(8,128)(2,1)}, bf16[2,144,1728]{2,1,0:T(8,128)(2,1)S(1)}, u32[]{:S(2)}, u32[]{:S(2)}) %collective-permute-start.12) | collective-permute-done | bytes 995360 | tf_op jit(solution)/shard_map/ppermute | solution.py:25
  57.7 53.4 %collective-permute-done.13 = bf16[2,144,1728]{2,1,0:T(8,128)(2,1)S(1)} collective-permute-done((bf16[2,144,1728]{2,1,0:T(8,128)(2,1)S(1)}, bf16[2,144,1728]{2,1,0:T(8,128)(2,1)S(1)}, u32[]{:S(2)}, u32[]{:S(2)}) %collective-permute-start.13) | collective-permute-done | bytes 995360 | tf_op jit(solution)/shard_map/ppermute | solution.py:25
  115.9 40.9 %collective-permute-done.14 = bf16[2,144,1728]{2,1,0:T(8,128)(2,1)} collective-permute-done((bf16[2,144,1728]{2,1,0:T(8,128)(2,1)S(1)}, bf16[2,144,1728]{2,1,0:T(8,128)(2,1)}, u32[]{:S(2)}, u32[]{:S(2)}) %collective-permute-start.14) | collective-permute-done | bytes 995360 | tf_op jit(solution)/shard_map/ppermute | solution.py:25
  164.5 21.9 %collective-permute-done = bf16[512]{0:T(512)(128)(2,1)S(1)} collective-permute-done((bf16[512]{0:T(512)(128)(2,1)S(1)}, bf16[512]{0:T(512)(128)(2,1)S(1)}, u32[]{:S(2)}, u32[]{:S(2)}) %collective-permute-start) | collective-permute-done | bytes 1056 | tf_op jit(solution)/shard_map/ppermute | solution.py:37
  187.6 6.3 collective-permute-done.15
  212.1 6.2 collective-permute-done.2
  233.0 8.0 %collective-permute-done.4 = bf16[512,256]{1,0:T(8,128)(2,1)S(1)} collective-permute-done((bf16[512,256]{1,0:T(8,128)(2,1)S(1)}, bf16[512,256]{1,0:T(8,128)(2,1)S(1)}, u32[]{:S(2)}, u32[]{:S(2)}) %collective-permute-start.4) | collective-permute-done | bytes 262176 | tf_op jit(solution)/shard_map/ppermute | solution.py:37
  242.5 6.5 collective-permute-done.5
  256.1 8.1 %gather_fusion = bf16[8,2,144,1728]{3,2,1,0:T(8,128)(2,1)} fusion(bf16[8,2,144,1728]{3,2,1,0:T(8,128)(2,1)} %bitcast_dynamic-update-slice_fusion, s32[1024]{0:T(1024)S(1)} %pad_clamp_fusion), kind=kCustom, calls=%fused_computation | custom fusion | bytes 15925280 | tf_op jit(solution)/shard_map/gather | solution.py:30
  289.7 6.4 multiply_convert_fusion.1
  304.9 6.0 collective-permute-done.21
  310.9 7.7 %collective-permute-done.20 = bf16[128,1152]{1,0:T(8,128)(2,1)S(1)} collective-permute-done((bf16[128,1152]{1,0:T(8,128)(2,1)S(1)}, bf16[128,1152]{1,0:T(8,128)(2,1)S(1)}, u32[]{:S(2)}, u32[]{:S(2)}) %collective-permute-start.20) | collective-permute-done | bytes 294944 | tf_op jit(solution)/shard_map/ppermute | solution.py:42
  322.8 6.6 collective-permute-done.24
  334.5 6.6 multiply_convert_fusion
  360.7 6.5 copy.60
  367.2 6.4 copy.62
  379.5 6.5 copy.64
  386.1 7.4 collective-permute-done.26
  405.1 7.0 collective-permute-done.29
  420.8 14.5 %collective-permute-done.31 = bf16[512,256]{1,0:T(8,128)(2,1)S(1)} collective-permute-done((bf16[512,256]{1,0:T(8,128)(2,1)S(1)}, bf16[512,256]{1,0:T(8,128)(2,1)S(1)}, u32[]{:S(2)}, u32[]{:S(2)}) %collective-permute-start.31) | collective-permute-done | bytes 262176 | tf_op jit(solution)/shard_map/ppermute | solution.py:37
  466.4 89.0 %reduce-scatter.15.cloned.1.call-done = bf16[144,1728]{1,0:T(8,128)(2,1)} async-done(((bf16[1152,1728]{1,0:T(8,128)(2,1)}), bf16[144,1728]{1,0:T(8,128)(2,1)}) %reduce-scatter.15.cloned.1.call-update) | async-done | bytes 497680
  557.6 88.6 %reduce-scatter.17.cloned.1.call-done = bf16[144,1728]{1,0:T(8,128)(2,1)} async-done(((bf16[1152,1728]{1,0:T(8,128)(2,1)}), bf16[144,1728]{1,0:T(8,128)(2,1)}) %reduce-scatter.17.cloned.1.call-update) | async-done | bytes 497680
  659.4 63.3 %reduce-scatter.19.cloned.1.call-done = bf16[144,1152]{1,0:T(8,128)(2,1)} async-done(((bf16[1152,1152]{1,0:T(8,128)(2,1)}), bf16[144,1152]{1,0:T(8,128)(2,1)}) %reduce-scatter.19.cloned.1.call-update) | async-done | bytes 331792
  731.4 9.0 %collective-permute-done.37 = bf16[144,640]{0,1:T(8,128)(2,1)S(1)} collective-permute-done((bf16[144,640]{0,1:T(8,128)(2,1)S(1)}, bf16[144,640]{0,1:T(8,128)(2,1)S(1)}, u32[]{:S(2)}, u32[]{:S(2)}) %collective-permute-start.37) | collective-permute-done | bytes 184352 | tf_op jit(solution)/shard_map/ppermute | solution.py:42
  (382 shorter events, 214.8 us)
Async XLA Ops:
  7.2 194.4 %all-gather.3.cloned.1.call-start = ((), (), s32[]{:S(2)}) async-start(), calls=%async_computation.4 | async-start | bytes 2985984 | tf_op jit(solution)/shard_map/all_gather | solution.py:153
  13.1 283.0 %all-gather.5.cloned.1.call-start = ((), (), s32[]{:S(2)}) async-start(), calls=%async_computation.5 | async-start | bytes 4644864 | tf_op jit(solution)/shard_map/all_gather | solution.py:155
  13.2 39.8 %collective-permute-start.12 = (bf16[2,144,1728]{2,1,0:T(8,128)(2,1)}, bf16[2,144,1728]{2,1,0:T(8,128)(2,1)S(1)}, u32[]{:S(2)}, u32[]{:S(2)}) collective-permute-start(bf16[2,144,1728]{2,1,0:T(8,128)(2,1)} %param.29), channel_id=1, source_target_pairs={{0,4},{4,8},{8,12},{12,16},{16,20},{20,24},{24,28},{28,0},{1,5},{5... | collective-permute-start | bytes 2985992 | tf_op jit(solution)/shard_map/ppermute | solution.py:25
  53.0 58.1 %collective-permute-start.13 = (bf16[2,144,1728]{2,1,0:T(8,128)(2,1)S(1)}, bf16[2,144,1728]{2,1,0:T(8,128)(2,1)S(1)}, u32[]{:S(2)}, u32[]{:S(2)}) collective-permute-start(bf16[2,144,1728]{2,1,0:T(8,128)(2,1)S(1)} %collective-permute-done.12), channel_id=1, source_target_pairs={{0,4},{4,8},{8,12},{12,16},{16,20},{20,24},{24,28},{28,0},{1,5},{5... | collective-permute-start | bytes 2985992 | tf_op jit(solution)/shard_map/ppermute | solution.py:25
  53.0 60.6 %collective-permute-start.16 = (bf16[2,144,1728]{2,1,0:T(8,128)(2,1)}, bf16[2,144,1728]{2,1,0:T(8,128)(2,1)S(1)}, u32[]{:S(2)}, u32[]{:S(2)}) collective-permute-start(bf16[2,144,1728]{2,1,0:T(8,128)(2,1)} %param.29), channel_id=1, source_target_pairs={{4,0},{8,4},{12,8},{16,12},{20,16},{24,20},{28,24},{0,28},{5,1},{9... | collective-permute-start | bytes 2985992 | tf_op jit(solution)/shard_map/ppermute | solution.py:27
  111.1 45.6 %collective-permute-start.14 = (bf16[2,144,1728]{2,1,0:T(8,128)(2,1)S(1)}, bf16[2,144,1728]{2,1,0:T(8,128)(2,1)}, u32[]{:S(2)}, u32[]{:S(2)}) collective-permute-start(bf16[2,144,1728]{2,1,0:T(8,128)(2,1)S(1)} %collective-permute-done.13), channel_id=1, source_target_pairs={{0,4},{4,8},{8,12},{12,16},{16,20},{20,24},{24,28},{28,0},{1,5},{5... | collective-permute-start | bytes 2985992 | tf_op jit(solution)/shard_map/ppermute | solution.py:25
  113.6 72.8 %collective-permute-start.17 = (bf16[2,144,1728]{2,1,0:T(8,128)(2,1)S(1)}, bf16[2,144,1728]{2,1,0:T(8,128)(2,1)}, u32[]{:S(2)}, u32[]{:S(2)}) collective-permute-start(bf16[2,144,1728]{2,1,0:T(8,128)(2,1)S(1)} %collective-permute-done.16), channel_id=1, source_target_pairs={{4,0},{8,4},{12,8},{16,12},{20,16},{24,20},{28,24},{0,28},{5,1},{9... | collective-permute-start | bytes 2985992 | tf_op jit(solution)/shard_map/ppermute | solution.py:27
  156.8 37.1 %collective-permute-start.15 = (bf16[2,144,1728]{2,1,0:T(8,128)(2,1)}, bf16[2,144,1728]{2,1,0:T(8,128)(2,1)}, u32[]{:S(2)}, u32[]{:S(2)}) collective-permute-start(bf16[2,144,1728]{2,1,0:T(8,128)(2,1)} %collective-permute-done.14), channel_id=1, source_target_pairs={{0,4},{4,8},{8,12},{12,16},{16,20},{20,24},{24,28},{28,0},{1,5},{5... | collective-permute-start | bytes 2985992 | tf_op jit(solution)/shard_map/ppermute | solution.py:25
  160.1 26.4 %collective-permute-start = (bf16[512]{0:T(512)(128)(2,1)S(1)}, bf16[512]{0:T(512)(128)(2,1)S(1)}, u32[]{:S(2)}, u32[]{:S(2)}) collective-permute-start(bf16[512]{0:T(512)(128)(2,1)S(1)} %add_convert_fusion.1), channel_id=1, source_target_pairs={{0,4},{4,8},{8,12},{12,16},{16,20},{20,24},{24,28},{1,5},{5,9},{9,... | collective-permute-start | bytes 3080 | tf_op jit(solution)/shard_map/ppermute | solution.py:37
  162.0 302.1 %reduce-scatter.13.cloned.1.call-start = ((), (), s32[]{:S(2)}) async-start(), calls=%async_computation.6 | async-start | bytes 4644864
  186.5 67.4 %collective-permute-start.18 = (bf16[2,144,1728]{2,1,0:T(8,128)(2,1)}, bf16[2,144,1728]{2,1,0:T(8,128)(2,1)}, u32[]{:S(2)}, u32[]{:S(2)}) collective-permute-start(bf16[2,144,1728]{2,1,0:T(8,128)(2,1)} %collective-permute-done.17), channel_id=1, source_target_pairs={{4,0},{8,4},{12,8},{16,12},{20,16},{24,20},{28,24},{0,28},{5,1},{9... | collective-permute-start | bytes 2985992 | tf_op jit(solution)/shard_map/ppermute | solution.py:27
  225.1 15.9 %collective-permute-start.4 = (bf16[512,256]{1,0:T(8,128)(2,1)S(1)}, bf16[512,256]{1,0:T(8,128)(2,1)S(1)}, u32[]{:S(2)}, u32[]{:S(2)}) collective-permute-start(bf16[512,256]{1,0:T(8,128)(2,1)S(1)} %pad_maximum_fusion.9), channel_id=1, source_target_pairs={{0,4},{4,8},{8,12},{12,16},{16,20},{20,24},{24,28},{1,5},{5,9},{9,... | collective-permute-start | bytes 786440 | tf_op jit(solution)/shard_map/ppermute | solution.py:37
  228.7 20.2 %collective-permute-start.5 = (bf16[512,256]{1,0:T(8,128)(2,1)S(1)}, bf16[512,256]{1,0:T(8,128)(2,1)S(1)}, u32[]{:S(2)}, u32[]{:S(2)}) collective-permute-start(bf16[512,256]{1,0:T(8,128)(2,1)S(1)} %slice.315), channel_id=1, source_target_pairs={{0,4},{4,8},{8,12},{12,16},{16,20},{20,24},{24,28},{1,5},{5,9},{9,... | collective-permute-start | bytes 786440 | tf_op jit(solution)/shard_map/ppermute | solution.py:37
  252.5 15.4 %collective-permute-start.7 = (bf16[128,1152]{1,0:T(8,128)(2,1)S(1)}, bf16[128,1152]{1,0:T(8,128)(2,1)}, u32[]{:S(2)}, u32[]{:S(2)}) collective-permute-start(bf16[128,1152]{1,0:T(8,128)(2,1)S(1)} %get-tuple-element.161), channel_id=1, source_target_pairs={{0,2},{1,3},{2,0},{3,1},{4,6},{5,7},{6,4},{7,5},{8,10},{9,11},{10,... | collective-permute-start | bytes 884744 | tf_op jit(solution)/shard_map/ppermute | solution.py:42
  253.8 14.3 %collective-permute-start.6 = (bf16[128,1152]{1,0:T(8,128)(2,1)S(1)}, bf16[128,1152]{1,0:T(8,128)(2,1)}, u32[]{:S(2)}, u32[]{:S(2)}) collective-permute-start(bf16[128,1152]{1,0:T(8,128)(2,1)S(1)} %get-tuple-element.159), channel_id=1, source_target_pairs={{0,1},{1,2},{2,3},{3,0},{4,5},{5,6},{6,7},{7,4},{8,9},{9,10},{10,1... | collective-permute-start | bytes 884744 | tf_op jit(solution)/shard_map/ppermute | solution.py:42
  303.6 15.0 %collective-permute-start.20 = (bf16[128,1152]{1,0:T(8,128)(2,1)S(1)}, bf16[128,1152]{1,0:T(8,128)(2,1)S(1)}, u32[]{:S(2)}, u32[]{:S(2)}) collective-permute-start(bf16[128,1152]{1,0:T(8,128)(2,1)S(1)} %get-tuple-element.158), channel_id=1, source_target_pairs={{0,2},{1,3},{2,0},{3,1},{4,6},{5,7},{6,4},{7,5},{8,10},{9,11},{10,... | collective-permute-start | bytes 884744 | tf_op jit(solution)/shard_map/ppermute | solution.py:42
  367.2 188.2 %reduce-scatter.15.cloned.1.call-start = ((), (), s32[]{:S(2)}) async-start(), calls=%async_computation.7 | async-start | bytes 4644864
  373.7 272.5 %reduce-scatter.17.cloned.1.call-start = ((), (), s32[]{:S(2)}) async-start(), calls=%async_computation.8 | async-start | bytes 4644864
  378.1 15.3 %collective-permute-start.26 = (bf16[128,1152]{1,0:T(8,128)(2,1)}, bf16[128,1152]{1,0:T(8,128)(2,1)}, u32[]{:S(2)}, u32[]{:S(2)}) collective-permute-start(bf16[128,1152]{1,0:T(8,128)(2,1)} %get-tuple-element.155), channel_id=1, source_target_pairs={{0,2},{1,3},{2,0},{3,1},{4,6},{5,7},{6,4},{7,5},{8,10},{9,11},{10,... | collective-permute-start | bytes 884744 | tf_op jit(solution)/shard_map/ppermute | solution.py:42
  386.0 336.7 %reduce-scatter.19.cloned.1.call-start = ((), (), s32[]{:S(2)}) async-start(), calls=%async_computation.9 | async-start | bytes 2985984
  414.2 23.4 %collective-permute-start.32 = (bf16[512,256]{1,0:T(8,128)(2,1)S(1)}, bf16[512,256]{1,0:T(8,128)(2,1)S(1)}, u32[]{:S(2)}, u32[]{:S(2)}) collective-permute-start(bf16[512,256]{1,0:T(8,128)(2,1)S(1)} %slice.313), channel_id=1, source_target_pairs={{4,0},{8,4},{12,8},{16,12},{20,16},{24,20},{28,24},{5,1},{9,5},{13... | collective-permute-start | bytes 786440 | tf_op jit(solution)/shard_map/ppermute | solution.py:37
  417.6 17.7 %collective-permute-start.31 = (bf16[512,256]{1,0:T(8,128)(2,1)S(1)}, bf16[512,256]{1,0:T(8,128)(2,1)S(1)}, u32[]{:S(2)}, u32[]{:S(2)}) collective-permute-start(bf16[512,256]{1,0:T(8,128)(2,1)S(1)} %slice.314), channel_id=1, source_target_pairs={{4,0},{8,4},{12,8},{16,12},{20,16},{24,20},{28,24},{5,1},{9,5},{13... | collective-permute-start | bytes 786440 | tf_op jit(solution)/shard_map/ppermute | solution.py:37
  723.9 16.4 %collective-permute-start.37 = (bf16[144,640]{0,1:T(8,128)(2,1)S(1)}, bf16[144,640]{0,1:T(8,128)(2,1)S(1)}, u32[]{:S(2)}, u32[]{:S(2)}) collective-permute-start(bf16[144,640]{0,1:T(8,128)(2,1)S(1)} %copy.69), channel_id=1, source_target_pairs={{0,2},{1,3},{2,0},{3,1},{4,6},{5,7},{6,4},{7,5},{8,10},{9,11},{10,... | collective-permute-start | bytes 552968 | tf_op jit(solution)/shard_map/ppermute | solution.py:42
  725.2 15.5 %collective-permute-start.36 = (bf16[144,640]{0,1:T(8,128)(2,1)S(1)}, bf16[144,640]{0,1:T(8,128)(2,1)S(1)}, u32[]{:S(2)}, u32[]{:S(2)}) collective-permute-start(bf16[144,640]{0,1:T(8,128)(2,1)S(1)} %copy.69), channel_id=1, source_target_pairs={{0,1},{1,2},{2,3},{3,0},{4,5},{5,6},{6,7},{7,4},{8,9},{9,10},{10,1... | collective-permute-start | bytes 552968 | tf_op jit(solution)/shard_map/ppermute | solution.py:42
  (103 other events, 1026.5 us)
Sparse Core Ops, SparseCore 0:
  13.3 101.8 all-gather.2
  162.1 95.8 all-gather.4
  367.3 96.7 reduce-scatter.12
  467.9 87.3 reduce-scatter.14
  558.8 87.3 reduce-scatter.16
  651.9 70.8 reduce-scatter.18
